TPU v7x, 32 devices: a whole 2x2x4 slice. The times are simulated.
32 devices in a mesh: dom: 4 (over y, core), mem: 8 (over z, x).
Axes of the slice: x: 2, y: 2, z: 4, core: 2. Of those that a mesh axis runs over, the one named last changes fastest.
Arguments:
- control: bfloat16 [64, 128, 8192], P('mem', None, 'dom'), may hold values from -6 to 6
- corr_offsets: int32 [64, 4], P('dom'), may hold values from -2 to 2, as said below
- corr_blocks: bfloat16 [64, 4, 128, 128], P('dom'), may hold values from -0.25 to 0.25
- interp_index: int32 [64, 4], P('dom'), may hold values from 0 to 15
- interp_blocks: bfloat16 [64, 4, 128, 128], P('dom'), may hold values from -0.25 to 0.25
- perturbations: bfloat16 [64, 128, 8192], P('mem', None, 'dom'), may hold values from -6 to 6
Outputs:
- increment: bfloat16 [128, 8192], P(None, 'dom')
Inputs may be any that keep to these rules, and one draw needn't show every extreme that they name: `corr_offsets`: each row holds 4 distinct offsets, among them 0, -2 and 2; exactly one of -1 and 1 is absent from each row. `interp_index`: an entry names a subgrid block of the tile that owns the column block, counted from that tile's first block.
All inputs are finite; a program needn't handle non-finite values.
Results may differ from a plain program's by a relative error of at most 0.0049.
Values may be sent and summed in bfloat16 or wider, within the bound.
A program may use at most 128 MiB of HBM per device.

v0:
```python
import jax
import jax.numpy as jnp
from jax import lax
from jax.sharding import PartitionSpec as P

HR = 2


def extended_2(block, sides, width):
    for axis, dim in sides:
        count = lax.axis_size(axis)
        forward = [(i, i + 1) for i in range(count - 1)]
        forward.append((count - 1, 0))
        backward = [(target, source) for source, target in forward]
        low = lax.ppermute(
            lax.slice_in_dim(block, block.shape[dim] - width, None, axis=dim), axis, forward
        )
        high = lax.ppermute(lax.slice_in_dim(block, 0, width, axis=dim), axis, backward)
        block = jnp.concatenate([low, block, high], axis=dim)
    return block


def smooth_blocks(control, corr_offsets, corr_blocks):
    members = control.shape[0]
    levels = control.shape[1]
    blocks = corr_blocks.shape[0]
    breadth = corr_blocks.shape[2]
    extended = extended_2(control, (("dom", 2),), HR * breadth)
    tile_rows = extended.reshape(members * levels, blocks + 2 * HR, breadth)
    source = jnp.arange(blocks, dtype=jnp.int32)[:, None] + HR + corr_offsets
    picked = tile_rows[:, source]
    smoothed = jnp.einsum("rbsj,bsji->rbi", picked, corr_blocks, preferred_element_type=jnp.float32)
    return smoothed.astype(jnp.bfloat16).reshape(members, levels, blocks, breadth)


def member_terms(smoothed, interp_index, interp_blocks, perturbations, level_count):
    members = smoothed.shape[0]
    blocks = smoothed.shape[2]
    breadth = smoothed.shape[3]
    column_blocks = interp_blocks.shape[0]
    feeding = smoothed.reshape(members * level_count, blocks, breadth)[:, interp_index]
    spread = jnp.einsum(
        "rqkj,qkji->rqi", feeding, interp_blocks, preferred_element_type=jnp.float32
    )
    spread = spread.reshape(members, level_count, column_blocks * breadth)
    return jnp.sum(perturbations.astype(jnp.float32) * spread, axis=0)


def per_device(control, corr_offsets, corr_blocks, interp_index, interp_blocks, perturbations):
    smoothed = smooth_blocks(control, corr_offsets, corr_blocks)
    levels = control.shape[1]
    members_all = control.shape[0] * lax.axis_size("mem")
    factor = 1.0 / jnp.sqrt(jnp.float32(members_all - 1))
    local_sum = member_terms(smoothed, interp_index, interp_blocks, perturbations, levels)
    summed = lax.psum(local_sum, "mem")
    return (summed * factor).astype(jnp.bfloat16)


def solution(mesh):
    in_specs = (
        P("mem", None, "dom"),
        P("dom", None),
        P("dom", None, None, None),
        P("dom", None),
        P("dom", None, None, None),
        P("mem", None, "dom"),
    )
    out_specs = P(None, "dom")
    return jax.shard_map(
        per_device, mesh=mesh, in_specs=in_specs, out_specs=out_specs, check_vma=False
    )
```

profile of v0, /device:TPU:0, one launch (start us, length us, event | category | flops | bytes accessed | tf_op | source)
XLA Modules:
  0.0 207.6 jit_solution(15530009346024782579)
XLA Ops:
  6.5 0.0 copy-start
  6.5 0.0 all-reduce.2.cloned.1.call-start
  6.5 2.4 %fusion.1 = (bf16[8,128,256]{2,1,0:T(8,128)(2,1)}, bf16[8,128,256]{2,1,0:T(8,128)(2,1)}) fusion(bf16[8,128,2048]{2,1,0:T(8,128)(2,1)} %param.6), kind=kLoop, calls=%fused_computation.13 | loop fusion | bytes 2097152 | tf_op jit(solution)/shard_map/slice | solution.py:16
  9.0 0.5 collective-permute-start
  9.4 2.0 collective-permute-start.1
  11.4 0.7 compare_select_fusion
  12.0 0.1 copy.13
  12.1 0.1 reshape.23
  12.2 0.7 compare_select_fusion.1
  12.9 0.1 copy.11
  13.0 0.1 reshape.15
  13.1 8.3 %collective-permute-done = bf16[8,128,256]{2,1,0:T(8,128)(2,1)S(1)} collective-permute-done((bf16[8,128,256]{2,1,0:T(8,128)(2,1)}, bf16[8,128,256]{2,1,0:T(8,128)(2,1)S(1)}, u32[]{:S(2)}, u32[]{:S(2)}) %collective-permute-start) | collective-permute-done | bytes 524320 | tf_op jit(solution)/shard_map/ppermute | solution.py:15
  21.4 2.6 %collective-permute-done.1 = bf16[8,128,256]{2,1,0:T(8,128)(2,1)S(1)} collective-permute-done((bf16[8,128,256]{2,1,0:T(8,128)(2,1)}, bf16[8,128,256]{2,1,0:T(8,128)(2,1)S(1)}, u32[]{:S(2)}, u32[]{:S(2)}) %collective-permute-start.1) | collective-permute-done | bytes 524320 | tf_op jit(solution)/shard_map/ppermute | solution.py:18
  24.0 5.0 %pad_maximum_fusion = bf16[8,128,2560]{2,1,0:T(8,128)(2,1)} fusion(bf16[8,128,256]{2,1,0:T(8,128)(2,1)S(1)} %collective-permute-done.1, bf16[8,128,2048]{2,1,0:T(8,128)(2,1)} %param.6, bf16[8,128,256]{2,1,0:T(8,128)(2,1)S(1)} %collective-permute-done), kind=kLoop, calls=%fused_computation.4 | loop fusion | flops 15728640 | bytes 10485760 | tf_op jit(solution)/shard_map/concatenate | solution.py:19
  29.0 10.0 %reshape.35 = bf16[1024,20,128]{2,1,0:T(8,128)(2,1)} reshape(bf16[8,128,2560]{2,1,0:T(8,128)(2,1)} %pad_maximum_fusion) | data formatting | bytes 10485760 | tf_op jit(solution)/shard_map/reshape | solution.py:29
  38.9 6.2 %copy.12 = bf16[1024,20,128]{2,0,1:T(8,128)(2,1)} copy(bf16[1024,20,128]{2,1,0:T(8,128)(2,1)} %reshape.35) | data formatting | bytes 10485760 | tf_op jit(solution)/shard_map/reshape | solution.py:29
  45.1 10.1 %gather_fusion = bf16[64,1024,128]{2,1,0:T(8,128)(2,1)} fusion(bf16[1024,20,128]{2,0,1:T(8,128)(2,1)} %copy.12, s32[1024]{0:T(1024)S(1)} %pad_clamp_fusion.1), kind=kCustom, calls=%fused_computation | custom fusion | bytes 33554688 | tf_op jit(solution)/shard_map/gather | solution.py:31
  55.2 0.0 copy-done
  55.2 12.2 %fusion = bf16[1024,16,128]{2,0,1:T(8,128)(2,1)} fusion(bf16[1024,16,4,128]{3,0,2,1:T(8,128)(2,1)} %bitcast.22, bf16[16,4,128,128]{3,2,1,0:T(8,128)(2,1)S(1)} %copy-done), kind=kOutput, calls=%fused_computation.5 | convolution fusion | flops 2149580800 | bytes 23068672 | tf_op jit(solution)/shard_map/rbsj,bsji->rbi/dot_general | solution.py:32
  67.5 0.0 copy-start.2
  67.5 9.9 %gather_fusion.1 = bf16[64,1024,128]{2,1,0:T(8,128)(2,1)} fusion(bf16[1024,16,128]{2,0,1:T(8,128)(2,1)} %fusion, s32[1024]{0:T(1024)S(1)} %pad_clamp_fusion), kind=kCustom, calls=%fused_computation.1 | custom fusion | bytes 33554688 | tf_op jit(solution)/shard_map/gather | solution.py:41
  77.3 0.0 copy-done.2
  77.3 13.5 %convolution_bitcast_fusion = f32[1024,16,128]{2,0,1:T(8,128)} fusion(bf16[1024,16,4,128]{3,0,2,1:T(8,128)(2,1)} %bitcast.23, bf16[16,4,128,128]{3,2,1,0:T(8,128)(2,1)S(1)} %copy-done.2), kind=kOutput, calls=%fused_computation.6 | convolution fusion | flops 2147483648 | bytes 27262976 | tf_op jit(solution)/shard_map/rqkj,qkji->rqi/dot_general | solution.py:42
  90.8 11.5 %copy.14 = f32[1024,16,128]{2,1,0:T(8,128)} copy(f32[1024,16,128]{2,0,1:T(8,128)} %convolution_bitcast_fusion) | data formatting | bytes 16777216 | tf_op jit(solution)/shard_map/rqkj,qkji->rqi/transpose | solution.py:42
  102.3 0.0 copy-start.1
  102.3 9.4 %reshape.12 = f32[8,128,2048]{2,1,0:T(8,128)} reshape(f32[1024,16,128]{2,1,0:T(8,128)} %copy.14) | data formatting | bytes 16777216 | tf_op jit(solution)/shard_map/reshape | solution.py:45
  111.7 7.0 %multiply_reduce_fusion = f32[128,2048]{1,0:T(8,128)} fusion(f32[8,128,2048]{2,1,0:T(8,128)} %reshape.12, bf16[8,128,2048]{2,1,0:T(8,128)(2,1)} %param.11), kind=kLoop, calls=%fused_computation.3 | loop fusion | flops 6029312 | bytes 13631488 | tf_op jit(solution)/shard_map/reduce_sum | solution.py:46
  118.7 0.0 all-reduce.2.cloned.1.call-update
  118.7 80.0 %all-reduce.2.cloned.1.call-done = f32[128,2048]{1,0:T(8,128)} async-done(((f32[128,2048]{1,0:T(8,128)}), f32[128,2048]{1,0:T(8,128)}) %all-reduce.2.cloned.1.call-update) | async-done | bytes 1048592 | tf_op jit(solution)/shard_map/psum | solution.py:55
  198.7 2.1 %multiply_convert_fusion = bf16[128,2048]{1,0:T(8,128)(2,1)} fusion(f32[128,2048]{1,0:T(8,128)} %all-reduce.2.cloned.1.call-done), kind=kLoop, calls=%fused_computation.7 | loop fusion | flops 524288 | bytes 1572864 | tf_op jit(solution)/shard_map/convert_element_type | solution.py:56
  200.8 0.0 copy-done.1
  (3 shorter events, 0.0 us)
Async XLA Ops:
  6.5 48.7 %copy-start = (bf16[16,4,128,128]{3,2,1,0:T(8,128)(2,1)S(1)}, bf16[16,4,128,128]{3,2,1,0:T(8,128)(2,1)}, u32[]{:S(2)}) copy-start(bf16[16,4,128,128]{3,2,1,0:T(8,128)(2,1)} %param.8) | copy-start | bytes 6291460
  6.5 192.1 %all-reduce.2.cloned.1.call-start = ((), (), s32[]{:S(2)}) async-start(), calls=%async_computation | async-start | bytes 2097152 | tf_op jit(solution)/shard_map/psum | solution.py:55
  9.0 12.4 %collective-permute-start = (bf16[8,128,256]{2,1,0:T(8,128)(2,1)}, bf16[8,128,256]{2,1,0:T(8,128)(2,1)S(1)}, u32[]{:S(2)}, u32[]{:S(2)}) collective-permute-start(bf16[8,128,256]{2,1,0:T(8,128)(2,1)} %get-tuple-element.5), channel_id=1, source_target_pairs={{0,8},{8,16},{16,24},{24,0},{1,9},{9,17},{17,25},{25,1},{2,10},{10... | collective-permute-start | bytes 1572872 | tf_op jit(solution)/shard_map/ppermute | solution.py:15
  9.4 14.6 %collective-permute-start.1 = (bf16[8,128,256]{2,1,0:T(8,128)(2,1)}, bf16[8,128,256]{2,1,0:T(8,128)(2,1)S(1)}, u32[]{:S(2)}, u32[]{:S(2)}) collective-permute-start(bf16[8,128,256]{2,1,0:T(8,128)(2,1)} %get-tuple-element.6), channel_id=1, source_target_pairs={{8,0},{16,8},{24,16},{0,24},{9,1},{17,9},{25,17},{1,25},{10,2},{18... | collective-permute-start | bytes 1572872 | tf_op jit(solution)/shard_map/ppermute | solution.py:18
  67.5 9.9 %copy-start.2 = (bf16[16,4,128,128]{3,2,1,0:T(8,128)(2,1)S(1)}, bf16[16,4,128,128]{3,2,1,0:T(8,128)(2,1)}, u32[]{:S(2)}) copy-start(bf16[16,4,128,128]{3,2,1,0:T(8,128)(2,1)} %param.10) | copy-start | bytes 6291460
  102.3 98.5 %copy-start.1 = (bf16[16,4,128,128]{3,2,1,0:T(8,128)(2,1)S(1)}, bf16[16,4,128,128]{3,2,1,0:T(8,128)(2,1)}, u32[]{:S(2)}) copy-start(bf16[16,4,128,128]{3,2,1,0:T(8,128)(2,1)} %param.8) | copy-start | bytes 6291460
Sparse Core Ops, SparseCore 0:
  118.8 79.8 all-reduce.1
where the time goes:
time: 208 us
  waiting for transfers between devices  90.8 us (44%)
  local copies, waits for them, and re-layouts  59.7 us (29%)
  matrix products  25.7 us (12%)
  other arithmetic  15.5 us (7%)
  between operations  13.4 us (6%)
  starting transfers between devices  2.41 us (1%)
    psum x1, waiting for transfers between devices, per_device(): summed = lax.psum(local_sum, 'mem')  80 us
    reshape x2, local copies, waits for them, and re-layouts, smooth_blocks(): tile_rows = extended.reshape(members * levels, blocks + 2 * HR, breadth)  16.1 us
    dot_general x1, matrix products, member_terms(): jnp.einsum('rqkj,qkji->rqi', feeding, interp_blocks, preferred_element_ty...  13.5 us
    dot_general x1, matrix products, smooth_blocks(): jnp.einsum('rbsj,bsji->rbi', picked, corr_blocks, preferred_element_type=...  12.2 us
    transpose x1, local copies, waits for them, and re-layouts, member_terms(): jnp.einsum('rqkj,qkji->rqi', feeding, interp_blocks, preferred_element_ty...  11.5 us
    gather x1, local copies, waits for them, and re-layouts, smooth_blocks(): picked = tile_rows[:, source]  10.1 us
    gather x1, local copies, waits for them, and re-layouts, member_terms(): smoothed.reshape(members * level_count, blocks, breadth)[:, interp_index]  9.85 us
    reshape x1, local copies, waits for them, and re-layouts, member_terms(): spread = spread.reshape(members, level_count, column_blocks * breadth)  9.4 us
  transfers between devices with their start and end apart: 3, of which 3 were waited for; matrix products, arithmetic and copies ran while one was open for 1% of the time, Pallas kernels for 0%

commit v1 on v0

v1 whole, which is shorter than its diff:
```python
import functools

import jax
import jax.numpy as jnp
from jax import lax
from jax.experimental import pallas as pl
from jax.experimental.pallas import tpu as pltpu
from jax.sharding import PartitionSpec as P

HR = 2
MESH = pl.DeviceIdType.MESH
RATE = 2


def chunk_sizes(levels):
    size = 32 if levels % 32 == 0 else levels
    return [size] * (levels // size)


def kernel(
    sizes, doms, mems,
    offs_ref, index_ref, control_ref, corr_ref, interp_ref, pert_ref,
    out_ref,
    *scratch,
):
    count = len(sizes)
    starts = [sum(sizes[:c]) for c in range(count)]
    bits = mems.bit_length() - 1
    halvings = bits - 1
    scratch = list(scratch)

    def take(n):
        got = scratch[:n]
        del scratch[:n]
        return got

    exts, smooths, perts = take(count), take(count), take(count)
    corr_v, interp_v, wide = take(3)
    txs = [take(bits) for _ in range(count)]
    rxs = [take(bits) for _ in range(count)]
    owns = [take(halvings) for _ in range(count)]
    load_sem, halo_send, halo_recv, red_send, red_recv, gat_send, gat_recv = take(7)

    members = control_ref.shape[0]
    blocks, stored, breadth = corr_ref.shape[0], corr_ref.shape[1], corr_ref.shape[2]
    column_blocks, feeds = interp_ref.shape[0], interp_ref.shape[1]
    width = blocks * breadth
    edge = HR * breadth
    pairs = blocks // 2

    me_dom = lax.axis_index("dom")
    me = lax.axis_index("mem")
    right = lax.rem(me_dom + 1, doms)
    left = lax.rem(me_dom + doms - 1, doms)
    bit = [lax.rem(me // (1 << s), 2) for s in range(bits)]
    partner = [me + (1 - 2 * bit[s]) * (1 << s) for s in range(bits)]

    def loaded(src, dst, slot):
        copy = pltpu.make_async_copy(src, dst, load_sem.at[slot])
        copy.start()
        return copy

    corr_load = loaded(corr_ref, corr_v, 0)
    control_loads = [
        loaded(
            control_ref.at[:, pl.ds(starts[c], sizes[c]), :],
            exts[c].at[:, :, pl.ds(edge, width)],
            2 + c,
        )
        for c in range(count)
    ]
    interp_load = loaded(interp_ref, interp_v, 1)
    pert_loads = [
        loaded(pert_ref.at[:, pl.ds(starts[c], sizes[c]), :], perts[c], 2 + count + c)
        for c in range(count)
    ]

    barrier = pltpu.get_barrier_semaphore()
    for neighbour in (left, right):
        pl.semaphore_signal(barrier, inc=1, device_id={"dom": neighbour}, device_id_type=MESH)
    for s in range(bits):
        pl.semaphore_signal(barrier, inc=1, device_id={"mem": partner[s]}, device_id_type=MESH)
    pl.semaphore_wait(barrier, 2 + bits)

    halos = []
    for c in range(count):
        rows = pl.ds(starts[c], sizes[c])
        pair = []
        for side, (src, dst, to) in enumerate(
            ((width - edge, 0, right), (0, edge + width, left))
        ):
            copy = pltpu.make_async_remote_copy(
                src_ref=control_ref.at[:, rows, pl.ds(src, edge)],
                dst_ref=exts[c].at[:, :, pl.ds(dst, edge)],
                send_sem=halo_send.at[2 * c + side],
                recv_sem=halo_recv.at[2 * c + side],
                device_id={"dom": to},
                device_id_type=MESH,
            )
            copy.start()
            pair.append(copy)
        halos.append(pair)

    corr_load.wait()

    def widen(p, carry):
        for r in range(2):
            b = 2 * p + r
            for j in range(2 + 2 * HR):
                shift = j - HR - r
                cell = (
                    p,
                    pl.ds(j * breadth, breadth),
                    pl.ds(r * breadth, breadth),
                )
                if abs(shift) > HR:
                    wide[cell] = jnp.zeros((breadth, breadth), wide.dtype)
                    continue
                slot = jnp.int32(0)
                found = jnp.int32(0)
                for s in range(stored):
                    here = offs_ref[s, b] == shift
                    slot = jnp.where(here, s, slot)
                    found = jnp.where(here, 1, found)
                value = corr_v[b, slot]
                if abs(shift) == 1:
                    value = value * found.astype(jnp.float32).astype(value.dtype)
                wide[cell] = value
        return carry

    lax.fori_loop(0, pairs, widen, 0)

    def smooth(c, p):
        rows = members * sizes[c]
        lhs = exts[c][:, :, pl.ds(pl.multiple_of(2 * p * breadth, breadth), (2 + 2 * HR) * breadth)]
        got = jnp.dot(
            lhs.reshape(rows, (2 + 2 * HR) * breadth), wide[p], preferred_element_type=jnp.float32
        ).astype(smooths[c].dtype)
        smooths[c][2 * p] = got[:, :breadth]
        smooths[c][2 * p + 1] = got[:, breadth:]

    for c in range(count):
        control_loads[c].wait()

        def inner(p, carry, c=c):
            smooth(c, p)
            return carry

        lax.fori_loop(1, pairs - 1, inner, 0, unroll=2)

    def columns(c, q):
        rows = members * sizes[c]
        lhs = jnp.concatenate(
            [smooths[c][index_ref[k, q]] for k in range(feeds)], axis=1
        )
        rhs = interp_v[q].reshape(feeds * breadth, breadth)
        spread = jnp.dot(lhs, rhs, preferred_element_type=jnp.float32)
        spread = spread.reshape(members, sizes[c], breadth)
        at = pl.ds(pl.multiple_of(q * breadth, breadth), breadth)
        return jnp.sum(perts[c][:, :, at].astype(jnp.float32) * spread, axis=0)

    def exchange(c, s):
        copy = pltpu.make_async_remote_copy(
            src_ref=txs[c][s],
            dst_ref=rxs[c][s],
            send_sem=red_send.at[c * bits + s],
            recv_sem=red_recv.at[c * bits + s],
            device_id={"mem": partner[s]},
            device_id_type=MESH,
        )
        copy.start()
        return copy

    half = [column_blocks >> (s + 1) for s in range(halvings)]
    held = [sum((bit[t] * half[t] for t in range(s + 1)), jnp.int32(0)) for s in range(halvings)]
    factor = 1.0 / jnp.sqrt(jnp.float32(members * mems - 1))
    reduces, gathers = {}, {}

    def compute(c):
        for copy in halos[c]:
            copy.wait_recv()
        if c == 0:
            interp_load.wait()
        pert_loads[c].wait()
        smooth(c, 0)
        smooth(c, pairs - 1)

        def away(j, carry):
            txs[c][0][j] = columns(c, (1 - bit[0]) * half[0] + j).astype(jnp.bfloat16)
            return carry

        def kept(j, carry):
            owns[c][0][j] = columns(c, bit[0] * half[0] + j)
            return carry

        lax.fori_loop(0, half[0], away, 0, unroll=2)
        reduces[c, 0] = exchange(c, 0)
        lax.fori_loop(0, half[0], kept, 0, unroll=2)

    def gather(c, s):
        place = out_ref.at[
            pl.ds(starts[c], sizes[c]),
            pl.ds(pl.multiple_of(held[s] * breadth, breadth), half[s] * breadth),
        ]
        copy = pltpu.make_async_remote_copy(
            src_ref=place,
            dst_ref=place,
            send_sem=gat_send.at[c * halvings + s],
            recv_sem=gat_recv.at[c * halvings + s],
            device_id={"mem": partner[s]},
            device_id_type=MESH,
        )
        copy.start()
        return copy

    def advance(c, stage):
        if stage < bits:
            reduces[c, stage].wait_recv()
        if stage < halvings - 1:
            size = half[stage + 1]
            send, keep = (1 - bit[stage + 1]) * size, bit[stage + 1] * size
            for i in range(size):
                txs[c][stage + 1][i] = (
                    owns[c][stage][send + i] + rxs[c][stage][send + i].astype(jnp.float32)
                ).astype(jnp.bfloat16)
            reduces[c, stage + 1] = exchange(c, stage + 1)
            for i in range(size):
                owns[c][stage + 1][i] = owns[c][stage][keep + i] + rxs[c][stage][
                    keep + i
                ].astype(jnp.float32)
        elif stage == halvings - 1:
            for i in range(half[stage]):
                txs[c][stage + 1][i] = (
                    owns[c][stage][i] + rxs[c][stage][i].astype(jnp.float32)
                ).astype(jnp.bfloat16)
            reduces[c, stage + 1] = exchange(c, stage + 1)
        elif stage == halvings:
            for i in range(half[-1]):
                total = txs[c][stage][i].astype(jnp.float32) + rxs[c][stage][i].astype(jnp.float32)
                at = pl.ds(pl.multiple_of((held[-1] + i) * breadth, breadth), breadth)
                out_ref[pl.ds(starts[c], sizes[c]), at] = (total * factor).astype(out_ref.dtype)
            gathers[c, halvings - 1] = gather(c, halvings - 1)
        else:
            s = 2 * halvings - stage
            gathers[c, s].wait_recv()
            if s > 0:
                gathers[c, s - 1] = gather(c, s - 1)

    steps = []
    for c in range(count):
        steps.append((RATE * c, 0, c, None))
        for stage in range(2 * halvings + 1):
            steps.append((RATE * (c + 1) + stage, 1, c, stage))
    for _, kind, c, stage in sorted(steps, key=lambda step: step[:3]):
        if kind == 0:
            compute(c)
        else:
            advance(c, stage)

    for pair in halos:
        for copy in pair:
            copy.wait_send()
    for key in sorted(reduces):
        reduces[key].wait_send()
    for key in sorted(gathers):
        gathers[key].wait_send()


def per_device(doms, mems, control, corr_offsets, corr_blocks, interp_index, interp_blocks, perturbations):
    members, levels, width = control.shape
    blocks, _, breadth, _ = corr_blocks.shape
    column_blocks = interp_blocks.shape[0]
    sizes = chunk_sizes(levels)
    count = len(sizes)
    bits = mems.bit_length() - 1
    halvings = bits - 1
    bf16, f32 = jnp.bfloat16, jnp.float32
    half = [column_blocks >> (s + 1) for s in range(halvings)]
    moved = half + [half[-1]]
    scratch = []
    scratch += [pltpu.VMEM((members, n, width + 2 * HR * breadth), bf16) for n in sizes]
    scratch += [pltpu.VMEM((blocks, members * n, breadth), bf16) for n in sizes]
    scratch += [pltpu.VMEM((members, n, perturbations.shape[2]), bf16) for n in sizes]
    scratch += [
        pltpu.VMEM(corr_blocks.shape, bf16),
        pltpu.VMEM(interp_blocks.shape, bf16),
        pltpu.VMEM((blocks // 2, (2 + 2 * HR) * breadth, 2 * breadth), bf16),
    ]
    for _ in range(2):
        scratch += [pltpu.VMEM((h, n, breadth), bf16) for n in sizes for h in moved]
    scratch += [pltpu.VMEM((h, n, breadth), f32) for n in sizes for h in half]
    scratch += [
        pltpu.SemaphoreType.DMA((2 + 2 * count,)),
        pltpu.SemaphoreType.DMA((2 * count,)),
        pltpu.SemaphoreType.DMA((2 * count,)),
        pltpu.SemaphoreType.DMA((count * bits,)),
        pltpu.SemaphoreType.DMA((count * bits,)),
        pltpu.SemaphoreType.DMA((count * halvings,)),
        pltpu.SemaphoreType.DMA((count * halvings,)),
    ]
    hbm = pl.BlockSpec(memory_space=pl.ANY)
    smem = pl.BlockSpec(memory_space=pltpu.SMEM)
    flops = 2 * members * levels * breadth * breadth * (6 * blocks + 4 * column_blocks)
    return pl.pallas_call(
        functools.partial(kernel, sizes, doms, mems),
        out_shape=jax.ShapeDtypeStruct((levels, column_blocks * breadth), bf16),
        in_specs=[smem, smem, hbm, hbm, hbm, hbm],
        out_specs=pl.BlockSpec(memory_space=pltpu.VMEM),
        scratch_shapes=scratch,
        compiler_params=pltpu.CompilerParams(
            collective_id=0, has_side_effects=True, vmem_limit_bytes=56 << 20
        ),
        cost_estimate=pl.CostEstimate(flops=flops, bytes_accessed=13 << 20, transcendentals=0),
    )(corr_offsets.T, interp_index.T, control, corr_blocks, interp_blocks, perturbations)


def solution(mesh):
    in_specs = (
        P("mem", None, "dom"),
        P("dom", None),
        P("dom", None, None, None),
        P("dom", None),
        P("dom", None, None, None),
        P("mem", None, "dom"),
    )
    out_specs = P(None, "dom")
    return jax.shard_map(
        functools.partial(per_device, mesh.shape["dom"], mesh.shape["mem"]),
        mesh=mesh, in_specs=in_specs, out_specs=out_specs, check_vma=False,
    )
```

time: 208 us -> 53.1 us (0.26)
  waiting for transfers between devices: 90.8 us -> 0 us
  local copies, waits for them, and re-layouts: 59.7 us -> 1.88 us
  Pallas kernels: 0 us -> 51 us
  matrix products: 25.7 us -> 0 us
  other arithmetic: 15.5 us -> 0 us
  between operations: 13.4 us -> 0.01 us
  starting transfers between devices: 2.41 us -> 0 us
    psum x1 -> x0, waiting for transfers between devices: 80 us -> none  [per_device(): summed = lax.psum(local_sum, 'mem')]
    pallas_call x0 -> x1, Pallas kernels: none -> 51 us  [per_device(): pl.pallas_call(functools.partial(kernel, sizes, doms, mems), out_shape=ja...]
    dot_general x2 -> x0, matrix products: 25.7 us -> none  [the longest x1 13.5 us: member_terms(): jnp.einsum('rqkj,qkji->rqi', feeding, interp_blocks, preferred_element_ty...]
    reshape x3 -> x0, local copies, waits for them, and re-layouts: 25.5 us -> none  [the longest x2 16.1 us: smooth_blocks(): tile_rows = extended.reshape(members * levels, blocks + 2 * HR, breadth)]
    gather x2 -> x0, local copies, waits for them, and re-layouts: 19.9 us -> none  [the longest x1 10.1 us: smooth_blocks(): picked = tile_rows[:, source]]
    transpose x1 -> x0, local copies, waits for them, and re-layouts: 11.5 us -> none  [member_terms(): jnp.einsum('rqkj,qkji->rqi', feeding, interp_blocks, preferred_element_ty...]
    ppermute x2 -> x0, waiting for transfers between devices: 10.9 us -> none  [the longest x1 8.26 us: extended_2(): lax.ppermute(lax.slice_in_dim(block, block.shape[dim] - width, None, axis...]
    reduce_sum x1 -> x0, other arithmetic: 7 us -> none  [member_terms(): return jnp.sum(perturbations.astype(jnp.float32) * spread, axis=0)]
  transfers between devices with their start and end apart: 3 -> 0, of which waited for: 3 -> 0; matrix products, arithmetic and copies ran while one was open for 1% -> 0% of each run, Pallas kernels for 0% -> 0%
where the time goes in v1:
time: 53.1 us; the launch traced here: 52.9 us
  Pallas kernels  51 us (96%)
  local copies, waits for them, and re-layouts  1.88 us (4%)
    pallas_call x1, Pallas kernels, per_device(): pl.pallas_call(functools.partial(kernel, sizes, doms, mems), out_shape=ja...  51 us
    unnamed x1, local copies, waits for them, and re-layouts  1.88 us

profile of v1, /device:TPU:0, one launch (start us, length us, event | category | flops | bytes accessed | tf_op | source)
XLA Modules:
  0.0 52.9 jit_solution(2469810768612908258)
XLA Ops:
  0.0 51.0 %shard_map.64 = bf16[128,2048]{1,0:T(8,128)(2,1)} custom-call(s32[4,16]{1,0:T(4,128)} %bitcast.2, s32[4,16]{1,0:T(4,128)} %bitcast.3, bf16[8,128,2048]{2,1,0:T(8,128)(2,1)} %control_ref.1, bf16[16,4,128,128]{3,2,1,0:T(8,128)(2,1)} %corr_ref.1, bf16[16,4,128,128]{3,2,1,0:T(8,128)(2,1)} %interp_ref.1, bf16[8,128,2048]{2,1,0:T(8,128)(2,1)} %pert_ref.1), custom_call_target="tpu_custom_call" | custom-call | flops 5368709120 | bytes 13631488 | tf_op jit(solution)/shard_map/pallas_call | solution.py:304
  51.0 1.9 %copy.8 = bf16[128,2048]{1,0:T(8,128)(2,1)} copy(bf16[128,2048]{1,0:T(8,128)(2,1)} %shard_map.64) | data formatting | bytes 1048576

commit v2 on v1

v2 whole, which is shorter than its diff:
```python
import functools

import jax
import jax.numpy as jnp
from jax import lax
from jax.experimental import pallas as pl
from jax.experimental.pallas import tpu as pltpu
from jax.sharding import PartitionSpec as P

HR = 2
MESH = pl.DeviceIdType.MESH
SIDE = 4


def chunk_sizes(levels):
    if levels % 32:
        return [levels]
    return [32] * (levels // 32 - 1) + [16, 16]


def kernel(
    sizes, doms, mems,
    offs_ref, index_ref, control_ref, corr_ref, interp_ref, pert_ref,
    out_ref,
    *scratch,
):
    count = len(sizes)
    starts = [sum(sizes[:c]) for c in range(count)]
    bits = mems.bit_length() - 1
    later = bits - 2
    peers = (3, 2, 1)
    scratch = list(scratch)

    def take(n):
        got = scratch[:n]
        del scratch[:n]
        return got

    exts, smooths, perts = take(count), take(count), take(count)
    corr_v, interp_v, wide = take(3)
    txs = [take(len(peers)) for _ in range(count)]
    rxs = [take(len(peers)) for _ in range(count)]
    sums_tx = [take(later) for _ in range(count)]
    sums_rx = [take(later) for _ in range(count)]
    owns, finals = take(count), take(count)
    load_sem, store_sem, halo_send, halo_recv = take(4)
    red_send, red_recv, sum_send, sum_recv, gat_send, gat_recv = take(6)

    members = control_ref.shape[0]
    blocks, stored, breadth = corr_ref.shape[0], corr_ref.shape[1], corr_ref.shape[2]
    column_blocks, feeds = interp_ref.shape[0], interp_ref.shape[1]
    width = blocks * breadth
    edge = HR * breadth
    pairs = blocks // 2

    me_dom = lax.axis_index("dom")
    me = lax.axis_index("mem")
    right = lax.rem(me_dom + 1, doms)
    left = lax.rem(me_dom + doms - 1, doms)
    bit = [lax.rem(me // (1 << s), 2) for s in range(bits)]

    def flipped(t):
        return me + sum((1 - 2 * bit[s]) * (1 << s) for s in range(bits) if (t >> s) & 1)

    def quarter(t):
        return lax.rem(flipped(t), SIDE) if t else lax.rem(me, SIDE)

    met = list(peers) + [1 << s for s in range(2, bits)]

    def loaded(src, dst, slot):
        copy = pltpu.make_async_copy(src, dst, load_sem.at[slot])
        copy.start()
        return copy

    corr_load = loaded(corr_ref, corr_v, 0)
    control_loads = [
        loaded(
            control_ref.at[:, pl.ds(starts[c], sizes[c]), :],
            exts[c].at[:, :, pl.ds(edge, width)],
            2 + c,
        )
        for c in range(count)
    ]
    interp_load = loaded(interp_ref, interp_v, 1)
    pert_loads = [
        loaded(pert_ref.at[:, pl.ds(starts[c], sizes[c]), :], perts[c], 2 + count + c)
        for c in range(count)
    ]

    barrier = pltpu.get_barrier_semaphore()
    for neighbour in (left, right):
        pl.semaphore_signal(barrier, inc=1, device_id={"dom": neighbour}, device_id_type=MESH)
    for t in met:
        pl.semaphore_signal(barrier, inc=1, device_id={"mem": flipped(t)}, device_id_type=MESH)
    pl.semaphore_wait(barrier, 2 + len(met))

    halos = []

    def send_halo():
        c = len(halos)
        if c == count:
            return
        rows = pl.ds(starts[c], sizes[c])
        pair = []
        for side, (src, dst, to) in enumerate(
            ((width - edge, 0, right), (0, edge + width, left))
        ):
            copy = pltpu.make_async_remote_copy(
                src_ref=control_ref.at[:, rows, pl.ds(src, edge)],
                dst_ref=exts[c].at[:, :, pl.ds(dst, edge)],
                send_sem=halo_send.at[2 * c + side],
                recv_sem=halo_recv.at[2 * c + side],
                device_id={"dom": to},
                device_id_type=MESH,
            )
            copy.start()
            pair.append(copy)
        halos.append(pair)

    def halo_left(c):
        for copy in halos[c]:
            copy.wait_send()

    send_halo()

    corr_load.wait()

    def widen(p, carry):
        for r in range(2):
            b = 2 * p + r
            for j in range(2 + 2 * HR):
                shift = j - HR - r
                cell = (
                    p,
                    pl.ds(j * breadth, breadth),
                    pl.ds(r * breadth, breadth),
                )
                if abs(shift) > HR:
                    wide[cell] = jnp.zeros((breadth, breadth), wide.dtype)
                    continue
                slot = jnp.int32(0)
                found = jnp.int32(0)
                for s in range(stored):
                    here = offs_ref[s, b] == shift
                    slot = jnp.where(here, s, slot)
                    found = jnp.where(here, 1, found)
                value = corr_v[b, slot]
                if abs(shift) == 1:
                    value = value * found.astype(jnp.float32).astype(value.dtype)
                wide[cell] = value
        return carry

    lax.fori_loop(0, pairs, widen, 0)
    send_halo()

    def smooth(c, p):
        rows = members * sizes[c]
        lhs = exts[c][:, :, pl.ds(pl.multiple_of(2 * p * breadth, breadth), (2 + 2 * HR) * breadth)]
        got = jnp.dot(
            lhs.reshape(rows, (2 + 2 * HR) * breadth), wide[p], preferred_element_type=jnp.float32
        ).astype(smooths[c].dtype)
        smooths[c][2 * p] = got[:, :breadth]
        smooths[c][2 * p + 1] = got[:, breadth:]

    for c in range(count):
        control_loads[c].wait()

        def inner(p, carry, c=c):
            smooth(c, p)
            return carry

        lax.fori_loop(1, pairs - 1, inner, 0, unroll=3)

    def columns(c, q):
        rows = members * sizes[c]
        lhs = jnp.concatenate(
            [smooths[c][index_ref[k, q]] for k in range(feeds)], axis=1
        )
        rhs = interp_v[q].reshape(feeds * breadth, breadth)
        spread = jnp.dot(lhs, rhs, preferred_element_type=jnp.float32)
        spread = spread.reshape(members, sizes[c], breadth)
        at = pl.ds(pl.multiple_of(q * breadth, breadth), breadth)
        return jnp.sum(perts[c][:, :, at].astype(jnp.float32) * spread, axis=0)

    def remote(src, dst, send, recv, t):
        copy = pltpu.make_async_remote_copy(
            src_ref=src, dst_ref=dst, send_sem=send, recv_sem=recv,
            device_id={"mem": flipped(t)}, device_id_type=MESH,
        )
        copy.start()
        return copy

    share = column_blocks // SIDE
    factor = 1.0 / jnp.sqrt(jnp.float32(members * mems - 1))
    reduces, exchanges, gathers, stores = {}, {}, {}, []

    def compute(c):
        for copy in halos[c]:
            copy.wait_recv()
        if c == 0:
            interp_load.wait()
        pert_loads[c].wait()
        smooth(c, 0)
        smooth(c, pairs - 1)
        if len(halos) < count:
            halo_left(c)
            send_halo()
        for n, t in enumerate(peers):
            def away(j, carry, n=n, t=t):
                txs[c][n][j] = columns(c, quarter(t) * share + j).astype(jnp.bfloat16)
                return carry

            lax.fori_loop(0, share, away, 0, unroll=True)
            at = c * len(peers) + n
            reduces[c, n] = remote(txs[c][n], rxs[c][n], red_send.at[at], red_recv.at[at], t)

        def kept(j, carry):
            owns[c][j] = columns(c, quarter(0) * share + j)
            return carry

        lax.fori_loop(0, share, kept, 0, unroll=True)

    def finish(c, j, total):
        at = pl.ds(j * breadth, breadth)
        finals[c][:, at] = (total * factor).astype(out_ref.dtype)

    def advance(c, stage):
        if stage == 0:
            for n in range(len(peers)):
                reduces[c, n].wait_recv()
        else:
            exchanges[c, stage - 1].wait_recv()
        for j in range(share):
            if stage == 0:
                total = owns[c][j]
                for n in range(len(peers)):
                    total = total + rxs[c][n][j].astype(jnp.float32)
            else:
                total = sums_tx[c][stage - 1][j].astype(jnp.float32) + sums_rx[c][stage - 1][
                    j
                ].astype(jnp.float32)
            if stage < later:
                sums_tx[c][stage][j] = total.astype(jnp.bfloat16)
            else:
                finish(c, j, total)
        if stage < later:
            at = c * later + stage
            exchanges[c, stage] = remote(
                sums_tx[c][stage], sums_rx[c][stage], sum_send.at[at], sum_recv.at[at], 1 << (stage + 2)
            )
            return
        place = out_ref.at[
            pl.ds(starts[c], sizes[c]),
            pl.ds(pl.multiple_of(quarter(0) * (share * breadth), breadth), share * breadth),
        ]
        for n, t in enumerate(peers):
            at = c * len(peers) + n
            gathers[c, n] = remote(finals[c], place, gat_send.at[at], gat_recv.at[at], t)
        store = pltpu.make_async_copy(finals[c], place, store_sem.at[c])
        store.start()
        stores.append(store)

    steps = [(c, 0, c, None) for c in range(count)]
    steps += [(c + 1 + stage, 1, c, stage) for c in range(count) for stage in range(later + 1)]
    for _, kind, c, stage in sorted(steps, key=lambda step: step[:3]):
        if kind == 0:
            compute(c)
        else:
            advance(c, stage)

    for c in range(max(count - 2, 0), count):
        halo_left(c)
    for group in (reduces, exchanges):
        for key in sorted(group):
            group[key].wait_send()
    for key in sorted(gathers):
        gathers[key].wait()
    for store in stores:
        store.wait()


def per_device(doms, mems, control, corr_offsets, corr_blocks, interp_index, interp_blocks, perturbations):
    members, levels, width = control.shape
    blocks, _, breadth, _ = corr_blocks.shape
    column_blocks = interp_blocks.shape[0]
    sizes = chunk_sizes(levels)
    count = len(sizes)
    later = mems.bit_length() - 3
    share = column_blocks // SIDE
    bf16, f32 = jnp.bfloat16, jnp.float32
    scratch = []
    scratch += [pltpu.VMEM((members, n, width + 2 * HR * breadth), bf16) for n in sizes]
    scratch += [pltpu.VMEM((blocks, members * n, breadth), bf16) for n in sizes]
    scratch += [pltpu.VMEM((members, n, perturbations.shape[2]), bf16) for n in sizes]
    scratch += [
        pltpu.VMEM(corr_blocks.shape, bf16),
        pltpu.VMEM(interp_blocks.shape, bf16),
        pltpu.VMEM((blocks // 2, (2 + 2 * HR) * breadth, 2 * breadth), bf16),
    ]
    for times in (SIDE - 1, SIDE - 1, later, later):
        scratch += [pltpu.VMEM((share, n, breadth), bf16) for n in sizes for _ in range(times)]
    scratch += [pltpu.VMEM((share, n, breadth), f32) for n in sizes]
    scratch += [pltpu.VMEM((n, share * breadth), bf16) for n in sizes]
    scratch += [
        pltpu.SemaphoreType.DMA((n,))
        for n in (2 + 2 * count, count, 2 * count, 2 * count, 3 * count, 3 * count)
        + (later * count, later * count, 3 * count, 3 * count)
    ]
    hbm = pl.BlockSpec(memory_space=pl.ANY)
    smem = pl.BlockSpec(memory_space=pltpu.SMEM)
    flops = 2 * members * levels * breadth * breadth * (6 * blocks + 4 * column_blocks)
    return pl.pallas_call(
        functools.partial(kernel, sizes, doms, mems),
        out_shape=jax.ShapeDtypeStruct((levels, column_blocks * breadth), bf16),
        in_specs=[smem, smem, hbm, hbm, hbm, hbm],
        out_specs=hbm,
        scratch_shapes=scratch,
        compiler_params=pltpu.CompilerParams(
            collective_id=0, has_side_effects=True, vmem_limit_bytes=56 << 20
        ),
        cost_estimate=pl.CostEstimate(flops=flops, bytes_accessed=13 << 20, transcendentals=0),
    )(corr_offsets.T, interp_index.T, control, corr_blocks, interp_blocks, perturbations)


def solution(mesh):
    in_specs = (
        P("mem", None, "dom"),
        P("dom", None),
        P("dom", None, None, None),
        P("dom", None),
        P("dom", None, None, None),
        P("mem", None, "dom"),
    )
    out_specs = P(None, "dom")
    return jax.shard_map(
        functools.partial(per_device, mesh.shape["dom"], mesh.shape["mem"]),
        mesh=mesh, in_specs=in_specs, out_specs=out_specs, check_vma=False,
    )
```

time: 53.1 us -> 40.7 us (0.77)
  Pallas kernels: 51 us -> 38.6 us
    pallas_call x1, Pallas kernels: 51 us -> 38.6 us  [per_device(): pl.pallas_call(functools.partial(kernel, sizes, doms, mems), out_shape=ja...]
where the time goes in v2:
time: 40.7 us; the launch traced here: 40.5 us
  Pallas kernels  38.6 us (95%)
  local copies, waits for them, and re-layouts  1.88 us (5%)
    pallas_call x1, Pallas kernels, per_device(): pl.pallas_call(functools.partial(kernel, sizes, doms, mems), out_shape=ja...  38.6 us
    unnamed x1, local copies, waits for them, and re-layouts  1.88 us

profile of v2, /device:TPU:0, one launch (start us, length us, event | category | flops | bytes accessed | tf_op | source)
XLA Modules:
  0.0 40.5 jit_solution(4929809234933946120)
XLA Ops:
  0.0 38.6 %shard_map.64 = bf16[128,2048]{1,0:T(8,128)(2,1)} custom-call(s32[4,16]{1,0:T(4,128)} %bitcast.2, s32[4,16]{1,0:T(4,128)} %bitcast.3, bf16[8,128,2048]{2,1,0:T(8,128)(2,1)} %control_ref.1, bf16[16,4,128,128]{3,2,1,0:T(8,128)(2,1)} %corr_ref.1, bf16[16,4,128,128]{3,2,1,0:T(8,128)(2,1)} %interp_ref.1, bf16[8,128,2048]{2,1,0:T(8,128)(2,1)} %pert_ref.1), custom_call_target="tpu_custom_call" | custom-call | flops 5368709120 | bytes 13631488 | tf_op jit(solution)/shard_map/pallas_call | solution.py:312
  38.7 1.9 %copy.8 = bf16[128,2048]{1,0:T(8,128)(2,1)} copy(bf16[128,2048]{1,0:T(8,128)(2,1)} %shard_map.64) | data formatting | bytes 1048576

commit v3 on v2

--- a/solution.py
+++ b/solution.py
@@ -13,9 +13,9 @@
 
 
 def chunk_sizes(levels):
-    if levels % 32:
+    if levels % 64:
         return [levels]
-    return [32] * (levels // 32 - 1) + [16, 16]
+    return [levels // 2] + [32] * (levels // 64)
 
 
 def kernel(
@@ -36,10 +36,9 @@
         del scratch[:n]
         return got
 
-    exts, smooths, perts = take(count), take(count), take(count)
-    corr_v, interp_v, wide = take(3)
-    txs = [take(len(peers)) for _ in range(count)]
-    rxs = [take(len(peers)) for _ in range(count)]
+    perts = take(count)
+    ext, smoothed, corr_v, interp_v, wide = take(5)
+    txs, rxs = take(count), take(count)
     sums_tx = [take(later) for _ in range(count)]
     sums_rx = [take(later) for _ in range(count)]
     owns, finals = take(count), take(count)
@@ -73,17 +72,18 @@
         return copy
 
     corr_load = loaded(corr_ref, corr_v, 0)
+    portion = control_ref.shape[1] // 2
     control_loads = [
         loaded(
-            control_ref.at[:, pl.ds(starts[c], sizes[c]), :],
-            exts[c].at[:, :, pl.ds(edge, width)],
-            2 + c,
+            control_ref.at[:, pl.ds(h * portion, portion), :],
+            ext.at[:, pl.ds(h * portion, portion), pl.ds(edge, width)],
+            2 + h,
         )
-        for c in range(count)
+        for h in range(2)
     ]
     interp_load = loaded(interp_ref, interp_v, 1)
     pert_loads = [
-        loaded(pert_ref.at[:, pl.ds(starts[c], sizes[c]), :], perts[c], 2 + count + c)
+        loaded(pert_ref.at[:, pl.ds(starts[c], sizes[c]), :], perts[c], 4 + c)
         for c in range(count)
     ]
 
@@ -107,7 +107,7 @@
         ):
             copy = pltpu.make_async_remote_copy(
                 src_ref=control_ref.at[:, rows, pl.ds(src, edge)],
-                dst_ref=exts[c].at[:, :, pl.ds(dst, edge)],
+                dst_ref=ext.at[:, rows, pl.ds(dst, edge)],
                 send_sem=halo_send.at[2 * c + side],
                 recv_sem=halo_recv.at[2 * c + side],
                 device_id={"dom": to},
@@ -153,28 +153,33 @@
     lax.fori_loop(0, pairs, widen, 0)
     send_halo()
 
-    def smooth(c, p):
-        rows = members * sizes[c]
-        lhs = exts[c][:, :, pl.ds(pl.multiple_of(2 * p * breadth, breadth), (2 + 2 * HR) * breadth)]
-        got = jnp.dot(
-            lhs.reshape(rows, (2 + 2 * HR) * breadth), wide[p], preferred_element_type=jnp.float32
-        ).astype(smooths[c].dtype)
-        smooths[c][2 * p] = got[:, :breadth]
-        smooths[c][2 * p + 1] = got[:, breadth:]
-
-    for c in range(count):
-        control_loads[c].wait()
-
-        def inner(p, carry, c=c):
-            smooth(c, p)
+    def smooth(start, size, p):
+        rows = pl.ds(start, size)
+        across = pl.ds(pl.multiple_of(2 * p * breadth, breadth), (2 + 2 * HR) * breadth)
+        lhs = ext[:, rows, across].reshape(members * size, (2 + 2 * HR) * breadth)
+        got = jnp.dot(lhs, wide[p], preferred_element_type=jnp.float32).astype(smoothed.dtype)
+        for r in range(2):
+            smoothed[2 * p + r, :, rows, :] = got[:, r * breadth : (r + 1) * breadth].reshape(
+                members, size, breadth
+            )
+
+    for h in range(2):
+        control_loads[h].wait()
+
+        def inner(p, carry, h=h):
+            smooth(h * portion, portion, p)
             return carry
 
-        lax.fori_loop(1, pairs - 1, inner, 0, unroll=3)
+        lax.fori_loop(1, pairs - 1, inner, 0)
 
     def columns(c, q):
         rows = members * sizes[c]
         lhs = jnp.concatenate(
-            [smooths[c][index_ref[k, q]] for k in range(feeds)], axis=1
+            [
+                smoothed[index_ref[k, q], :, pl.ds(starts[c], sizes[c]), :].reshape(rows, breadth)
+                for k in range(feeds)
+            ],
+            axis=1,
         )
         rhs = interp_v[q].reshape(feeds * breadth, breadth)
         spread = jnp.dot(lhs, rhs, preferred_element_type=jnp.float32)
@@ -194,31 +199,50 @@
     factor = 1.0 / jnp.sqrt(jnp.float32(members * mems - 1))
     reduces, exchanges, gathers, stores = {}, {}, {}, []
 
+    def scatter(c, n, to):
+        at = c * len(peers) + n
+        return pltpu.make_async_remote_copy(
+            src_ref=txs[c].at[n], dst_ref=rxs[c].at[n],
+            send_sem=red_send.at[at], recv_sem=red_recv.at[at],
+            device_id={"mem": to}, device_id_type=MESH,
+        )
+
     def compute(c):
         for copy in halos[c]:
             copy.wait_recv()
         if c == 0:
             interp_load.wait()
         pert_loads[c].wait()
-        smooth(c, 0)
-        smooth(c, pairs - 1)
+        smooth(starts[c], sizes[c], 0)
+        smooth(starts[c], sizes[c], pairs - 1)
         if len(halos) < count:
             halo_left(c)
             send_halo()
+        low, high = bit[0], bit[1]
+
+        def away(n, carry):
+            t = SIDE - 1 - n
+            t_low, t_high = lax.rem(t, 2), t // 2
+            u_low, u_high = low + t_low - 2 * low * t_low, high + t_high - 2 * high * t_high
+            owner = u_low + 2 * u_high
+
+            def one(j, inner):
+                txs[c][n, j] = columns(c, owner * share + j).astype(jnp.bfloat16)
+                return inner
+
+            lax.fori_loop(0, share, one, 0, unroll=2)
+            scatter(c, n, me + (u_low - low) + 2 * (u_high - high)).start()
+            return carry
+
+        lax.fori_loop(0, len(peers), away, 0)
         for n, t in enumerate(peers):
-            def away(j, carry, n=n, t=t):
-                txs[c][n][j] = columns(c, quarter(t) * share + j).astype(jnp.bfloat16)
-                return carry
-
-            lax.fori_loop(0, share, away, 0, unroll=True)
-            at = c * len(peers) + n
-            reduces[c, n] = remote(txs[c][n], rxs[c][n], red_send.at[at], red_recv.at[at], t)
+            reduces[c, n] = scatter(c, n, flipped(t))
 
         def kept(j, carry):
             owns[c][j] = columns(c, quarter(0) * share + j)
             return carry
 
-        lax.fori_loop(0, share, kept, 0, unroll=True)
+        lax.fori_loop(0, share, kept, 0, unroll=2)
 
     def finish(c, j, total):
         at = pl.ds(j * breadth, breadth)
@@ -234,7 +258,7 @@
             if stage == 0:
                 total = owns[c][j]
                 for n in range(len(peers)):
-                    total = total + rxs[c][n][j].astype(jnp.float32)
+                    total = total + rxs[c][n, j].astype(jnp.float32)
             else:
                 total = sums_tx[c][stage - 1][j].astype(jnp.float32) + sums_rx[c][stage - 1][
                     j
@@ -289,21 +313,23 @@
     share = column_blocks // SIDE
     bf16, f32 = jnp.bfloat16, jnp.float32
     scratch = []
-    scratch += [pltpu.VMEM((members, n, width + 2 * HR * breadth), bf16) for n in sizes]
-    scratch += [pltpu.VMEM((blocks, members * n, breadth), bf16) for n in sizes]
     scratch += [pltpu.VMEM((members, n, perturbations.shape[2]), bf16) for n in sizes]
     scratch += [
+        pltpu.VMEM((members, levels, width + 2 * HR * breadth), bf16),
+        pltpu.VMEM((blocks, members, levels, breadth), bf16),
         pltpu.VMEM(corr_blocks.shape, bf16),
         pltpu.VMEM(interp_blocks.shape, bf16),
         pltpu.VMEM((blocks // 2, (2 + 2 * HR) * breadth, 2 * breadth), bf16),
     ]
-    for times in (SIDE - 1, SIDE - 1, later, later):
+    for _ in range(2):
+        scratch += [pltpu.VMEM((SIDE - 1, share, n, breadth), bf16) for n in sizes]
+    for times in (later, later):
         scratch += [pltpu.VMEM((share, n, breadth), bf16) for n in sizes for _ in range(times)]
     scratch += [pltpu.VMEM((share, n, breadth), f32) for n in sizes]
     scratch += [pltpu.VMEM((n, share * breadth), bf16) for n in sizes]
     scratch += [
         pltpu.SemaphoreType.DMA((n,))
-        for n in (2 + 2 * count, count, 2 * count, 2 * count, 3 * count, 3 * count)
+        for n in (4 + count, count, 2 * count, 2 * count, 3 * count, 3 * count)
         + (later * count, later * count, 3 * count, 3 * count)
     ]
     hbm = pl.BlockSpec(memory_space=pl.ANY)

time: 40.7 us -> 40.8 us (level)
  no operation moved by 1% of the time
where the time goes in v3:
time: 40.8 us; the launch traced here: 40.6 us
  Pallas kernels  38.8 us (95%)
  local copies, waits for them, and re-layouts  1.88 us (5%)
    pallas_call x1, Pallas kernels, per_device(): pl.pallas_call(functools.partial(kernel, sizes, doms, mems), out_shape=ja...  38.8 us
    unnamed x1, local copies, waits for them, and re-layouts  1.88 us

profile of v3, /device:TPU:0, one launch (start us, length us, event | category | flops | bytes accessed | tf_op | source)
XLA Modules:
  0.0 40.6 jit_solution(14287595033209743661)
XLA Ops:
  0.0 38.8 %shard_map.64 = bf16[128,2048]{1,0:T(8,128)(2,1)} custom-call(s32[4,16]{1,0:T(4,128)} %bitcast.2, s32[4,16]{1,0:T(4,128)} %bitcast.3, bf16[8,128,2048]{2,1,0:T(8,128)(2,1)} %control_ref.1, bf16[16,4,128,128]{3,2,1,0:T(8,128)(2,1)} %corr_ref.1, bf16[16,4,128,128]{3,2,1,0:T(8,128)(2,1)} %interp_ref.1, bf16[8,128,2048]{2,1,0:T(8,128)(2,1)} %pert_ref.1), custom_call_target="tpu_custom_call" | custom-call | flops 5368709120 | bytes 13631488 | tf_op jit(solution)/shard_map/pallas_call | solution.py:338
  38.8 1.9 %copy.8 = bf16[128,2048]{1,0:T(8,128)(2,1)} copy(bf16[128,2048]{1,0:T(8,128)(2,1)} %shard_map.64) | data formatting | bytes 1048576

commit v4 on v3

--- a/solution.py
+++ b/solution.py
@@ -13,9 +13,9 @@
 
 
 def chunk_sizes(levels):
-    if levels % 64:
+    if levels % 32:
         return [levels]
-    return [levels // 2] + [32] * (levels // 64)
+    return [32] * (levels // 32)
 
 
 def kernel(
@@ -72,21 +72,6 @@
         return copy
 
     corr_load = loaded(corr_ref, corr_v, 0)
-    portion = control_ref.shape[1] // 2
-    control_loads = [
-        loaded(
-            control_ref.at[:, pl.ds(h * portion, portion), :],
-            ext.at[:, pl.ds(h * portion, portion), pl.ds(edge, width)],
-            2 + h,
-        )
-        for h in range(2)
-    ]
-    interp_load = loaded(interp_ref, interp_v, 1)
-    pert_loads = [
-        loaded(pert_ref.at[:, pl.ds(starts[c], sizes[c]), :], perts[c], 4 + c)
-        for c in range(count)
-    ]
-
     barrier = pltpu.get_barrier_semaphore()
     for neighbour in (left, right):
         pl.semaphore_signal(barrier, inc=1, device_id={"dom": neighbour}, device_id_type=MESH)
@@ -122,6 +107,20 @@
             copy.wait_send()
 
     send_halo()
+    portion = control_ref.shape[1] // 2
+    control_loads = [
+        loaded(
+            control_ref.at[:, pl.ds(h * portion, portion), :],
+            ext.at[:, pl.ds(h * portion, portion), pl.ds(edge, width)],
+            2 + h,
+        )
+        for h in range(2)
+    ]
+    interp_load = loaded(interp_ref, interp_v, 1)
+    pert_loads = [
+        loaded(pert_ref.at[:, pl.ds(starts[c], sizes[c]), :], perts[c], 4 + c)
+        for c in range(count)
+    ]
 
     corr_load.wait()
 

time: 40.8 us -> 40.8 us (level)
  no operation moved by 1% of the time
where the time goes in v4:
time: 40.8 us; the launch traced here: 40.7 us
  Pallas kernels  38.8 us (95%)
  local copies, waits for them, and re-layouts  1.88 us (5%)
    pallas_call x1, Pallas kernels, per_device(): pl.pallas_call(functools.partial(kernel, sizes, doms, mems), out_shape=ja...  38.8 us
    unnamed x1, local copies, waits for them, and re-layouts  1.88 us

profile of v4, /device:TPU:0, one launch (start us, length us, event | category | flops | bytes accessed | tf_op | source)
XLA Modules:
  0.0 40.7 jit_solution(10606054143051583551)
XLA Ops:
  0.0 38.8 %shard_map.64 = bf16[128,2048]{1,0:T(8,128)(2,1)} custom-call(s32[4,16]{1,0:T(4,128)} %bitcast.2, s32[4,16]{1,0:T(4,128)} %bitcast.3, bf16[8,128,2048]{2,1,0:T(8,128)(2,1)} %control_ref.1, bf16[16,4,128,128]{3,2,1,0:T(8,128)(2,1)} %corr_ref.1, bf16[16,4,128,128]{3,2,1,0:T(8,128)(2,1)} %interp_ref.1, bf16[8,128,2048]{2,1,0:T(8,128)(2,1)} %pert_ref.1), custom_call_target="tpu_custom_call" | custom-call | flops 5368709120 | bytes 13631488 | tf_op jit(solution)/shard_map/pallas_call | solution.py:337
  38.8 1.9 %copy.8 = bf16[128,2048]{1,0:T(8,128)(2,1)} copy(bf16[128,2048]{1,0:T(8,128)(2,1)} %shard_map.64) | data formatting | bytes 1048576

commit v5 on v4

--- a/solution.py
+++ b/solution.py
@@ -15,7 +15,7 @@
 def chunk_sizes(levels):
     if levels % 32:
         return [levels]
-    return [32] * (levels // 32)
+    return [32] * (levels // 32 - 1) + [16, 16]
 
 
 def kernel(
@@ -170,6 +170,10 @@
             return carry
 
         lax.fori_loop(1, pairs - 1, inner, 0)
+        send_halo()
+
+    while len(halos) < count:
+        send_halo()
 
     def columns(c, q):
         rows = members * sizes[c]
@@ -214,9 +218,6 @@
         pert_loads[c].wait()
         smooth(starts[c], sizes[c], 0)
         smooth(starts[c], sizes[c], pairs - 1)
-        if len(halos) < count:
-            halo_left(c)
-            send_halo()
         low, high = bit[0], bit[1]
 
         def away(n, carry):
@@ -291,7 +292,7 @@
         else:
             advance(c, stage)
 
-    for c in range(max(count - 2, 0), count):
+    for c in range(count):
         halo_left(c)
     for group in (reduces, exchanges):
         for key in sorted(group):

time: 40.8 us -> 42.2 us (1.034)
  Pallas kernels: 38.8 us -> 40.1 us
    pallas_call x1, Pallas kernels: 38.8 us -> 40.1 us  [per_device(): pl.pallas_call(functools.partial(kernel, sizes, doms, mems), out_shape=ja...]
where the time goes in v5:
time: 42.2 us; the launch traced here: 42 us
  Pallas kernels  40.1 us (95%)
  local copies, waits for them, and re-layouts  1.88 us (4%)
    pallas_call x1, Pallas kernels, per_device(): pl.pallas_call(functools.partial(kernel, sizes, doms, mems), out_shape=ja...  40.1 us
    unnamed x1, local copies, waits for them, and re-layouts  1.88 us

profile of v5, /device:TPU:0, one launch (start us, length us, event | category | flops | bytes accessed | tf_op | source)
XLA Modules:
  0.0 42.0 jit_solution(5854653562581269603)
XLA Ops:
  0.0 40.1 %shard_map.64 = bf16[128,2048]{1,0:T(8,128)(2,1)} custom-call(s32[4,16]{1,0:T(4,128)} %bitcast.2, s32[4,16]{1,0:T(4,128)} %bitcast.3, bf16[8,128,2048]{2,1,0:T(8,128)(2,1)} %control_ref.1, bf16[16,4,128,128]{3,2,1,0:T(8,128)(2,1)} %corr_ref.1, bf16[16,4,128,128]{3,2,1,0:T(8,128)(2,1)} %interp_ref.1, bf16[8,128,2048]{2,1,0:T(8,128)(2,1)} %pert_ref.1), custom_call_target="tpu_custom_call" | custom-call | flops 5368709120 | bytes 13631488 | tf_op jit(solution)/shard_map/pallas_call | solution.py:338
  40.1 1.9 %copy.8 = bf16[128,2048]{1,0:T(8,128)(2,1)} copy(bf16[128,2048]{1,0:T(8,128)(2,1)} %shard_map.64) | data formatting | bytes 1048576
